TPU v7x, 32 devices: a whole 2x2x4 slice. The times are simulated.
32 devices in a mesh: orb: 8 (over z, y), rep: 4 (over x, core).
Axes of the slice: x: 2, y: 2, z: 4, core: 2. Of those that a mesh axis runs over, the one named last changes fastest.
Arguments:
- blocks: bfloat16 [16, 1024, 512], P('orb', 'rep'), may hold values from -1.078125 to 1.078125
- amplitudes: bfloat16 [64, 512, 512], P('orb', 'rep'), may hold values from -3 to 3
- pair_orbitals: int32 [64, 2], P('orb'), may hold values from 0 to 15, as said below
- coupling: int32 [64, 4], P('orb'), may hold values from 0 to 63, as said below
- fock_coupling: bfloat16 [64, 4], P('orb'), may hold values from -0.5 to 0.5
- virtual_energy: float32 [512], replicated, may hold values from 0.3 to 2
- occupied_energy: float32 [16], replicated, may hold values from -1.5 to -0.1
Outputs:
- updated_amplitudes: bfloat16 [64, 512, 512], P('orb', 'rep')
Inputs may be any that keep to these rules, and one draw needn't show every extreme that they name: `pair_orbitals`: orbital o lives on owner o // 2 and pair p on owner p // 8. A pair's first orbital lies on the pair's owner; its second lies on the same owner or the next one. `coupling`: every coupled pair lies on the pair's owner or on an adjacent owner.
All inputs are finite; a program needn't handle non-finite values.
Results may differ from a plain program's by a relative error of at most 0.01.
Values may be sent and summed in bfloat16 or wider, within the bound.
A program may use at most 64 MiB of HBM per device.

v0:
```python
import jax
import jax.numpy as jnp
from jax import lax
from jax.sharding import PartitionSpec as P

damping = 0.7


def passed_along(block, axis, distance):
    devices = range(lax.axis_size(axis))
    route = [(i - distance, i) for i in devices if i - distance in devices]
    return lax.ppermute(block, axis, route)


def extended_2(x, sides, width):
    for axis, dim in sides:
        peers, length = (lax.axis_size(axis), x.shape[dim])
        up = [(i, (i + 1) % peers) for i in range(peers - 1)]
        down = [(j, i) for i, j in up]
        last = lax.slice_in_dim(x, length - width, length, axis=dim)
        leading = lax.slice_in_dim(x, 0, width, axis=dim)
        before = lax.ppermute(last, axis, up)
        after = lax.ppermute(leading, axis, down)
        x = jnp.concatenate([before, x, after], axis=dim)
    return x


def per_device(
    blocks, amplitudes, pair_orbitals, coupling, fock_coupling, virtual_energy, occupied_energy
):
    orbital_count = blocks.shape[0]
    pair_count = amplitudes.shape[0]
    row_count = amplitudes.shape[1]
    owner_index = lax.axis_index("orb")
    replica_index = lax.axis_index("rep")
    first_local = pair_orbitals[:, 0] - owner_index * orbital_count
    second_local = pair_orbitals[:, 1] - owner_index * orbital_count
    next_blocks = passed_along(blocks, "orb", -1)
    extended = jnp.concatenate([blocks, next_blocks], axis=0)
    whole_aux = lax.all_gather(extended, "rep", axis=1, tiled=True)
    groups = lax.axis_size("rep")
    quarter = whole_aux.shape[1] // groups
    full_rows = whole_aux.shape[2]
    own_rows = lax.dynamic_slice_in_dim(
        whole_aux[:orbital_count], replica_index * row_count, row_count, 2
    )
    left_split = own_rows.reshape(orbital_count, groups, quarter, row_count)
    right_split = whole_aux.reshape(2 * orbital_count, groups, quarter, full_rows)
    combos = jnp.einsum(
        "igqa,jgqb->ijgab", left_split, right_split, preferred_element_type=jnp.float32
    )
    rounded = combos.astype(jnp.bfloat16)
    picked_pairs = rounded[first_local, second_local]
    integrals = jnp.sum(picked_pairs.astype(jnp.float32), axis=1)
    amp_extended = extended_2(amplitudes, (("orb", 0),), pair_count)
    coupled_local = coupling - (owner_index - 1) * pair_count
    picked = amp_extended[coupled_local]
    coupled = jnp.einsum("pc,pcab->pab", fock_coupling, picked, preferred_element_type=jnp.float32)
    row_energy = lax.dynamic_slice_in_dim(virtual_energy, replica_index * row_count, row_count)
    orbital_ids = jnp.arange(occupied_energy.shape[0], dtype=jnp.int32)
    matches = (pair_orbitals[:, :, None] == orbital_ids[None, None, :]).astype(jnp.float32)
    pair_shift = jnp.sum(matches * occupied_energy[None, None, :], axis=(1, 2))
    denominator = (
        row_energy[None, :, None] + virtual_energy[None, None, :] - pair_shift[:, None, None]
    )
    residual = integrals - coupled
    updated = (1.0 - damping) * amplitudes.astype(jnp.float32) - damping * residual / denominator
    return updated.astype(jnp.bfloat16)


def solution(mesh):
    placed = (
        P("orb", "rep", None),
        P("orb", "rep", None),
        P("orb", None),
        P("orb", None),
        P("orb", None),
        P(),
        P(),
    )
    return jax.shard_map(
        per_device, mesh=mesh, in_specs=placed, out_specs=P("orb", "rep", None), check_vma=False
    )
```

profile of v0, /device:TPU:4, one launch (start us, length us, event | category | flops | bytes accessed | tf_op | source)
XLA Modules:
  0.0 111.2 jit_solution(10714368861135061677)
XLA Ops:
  6.6 2.1 %collective-permute-start = (bf16[2,256,512]{2,1,0:T(8,128)(2,1)}, bf16[2,256,512]{2,1,0:T(8,128)(2,1)S(1)}, u32[]{:S(2)}, u32[]{:S(2)}) collective-permute-start(bf16[2,256,512]{2,1,0:T(8,128)(2,1)} %param.7), channel_id=1, source_target_pairs={{4,0},{8,4},{12,8},{16,12},{20,16},{24,20},{28,24},{5,1},{9,5},{13... | collective-permute-start | bytes 1572872 | tf_op jit(solution)/shard_map/ppermute | solution.py:12
  8.7 14.7 %collective-permute-done = bf16[2,256,512]{2,1,0:T(8,128)(2,1)S(1)} collective-permute-done((bf16[2,256,512]{2,1,0:T(8,128)(2,1)}, bf16[2,256,512]{2,1,0:T(8,128)(2,1)S(1)}, u32[]{:S(2)}, u32[]{:S(2)}) %collective-permute-start) | collective-permute-done | bytes 524320 | tf_op jit(solution)/shard_map/ppermute | solution.py:12
  23.4 2.1 %pad_maximum_fusion.1 = bf16[4,256,512]{2,1,0:T(8,128)(2,1)} fusion(bf16[2,256,512]{2,1,0:T(8,128)(2,1)S(1)} %collective-permute-done, bf16[2,256,512]{2,1,0:T(8,128)(2,1)} %param.7), kind=kLoop, calls=%fused_computation.9 | loop fusion | flops 524288 | bytes 2097152 | tf_op jit(solution)/shard_map/concatenate | solution.py:39
  25.5 1.9 %collective-permute-start.2 = (bf16[8,128,512]{2,1,0:T(8,128)(2,1)S(1)}, bf16[8,128,512]{2,1,0:T(8,128)(2,1)S(1)}, u32[]{:S(2)}, u32[]{:S(2)}) collective-permute-start(bf16[8,128,512]{2,1,0:T(8,128)(2,1)S(1)} %copy-done), channel_id=1, source_target_pairs={{4,0},{8,4},{12,8},{16,12},{20,16},{24,20},{28,24},{5,1},{9,5},{13... | collective-permute-start | bytes 3145736 | tf_op jit(solution)/shard_map/ppermute | solution.py:23
  27.5 4.8 %collective-permute-start.1 = (bf16[8,128,512]{2,1,0:T(8,128)(2,1)S(1)}, bf16[8,128,512]{2,1,0:T(8,128)(2,1)}, u32[]{:S(2)}, u32[]{:S(2)}) collective-permute-start(bf16[8,128,512]{2,1,0:T(8,128)(2,1)S(1)} %copy-done), channel_id=1, source_target_pairs={{0,4},{4,8},{8,12},{12,16},{16,20},{20,24},{24,28},{1,5},{5,9},{9,... | collective-permute-start | bytes 3145736 | tf_op jit(solution)/shard_map/ppermute | solution.py:22
  32.3 1.3 %copy.20 = bf16[8,128,512]{1,2,0:T(8,128)(2,1)} copy(bf16[8,128,512]{2,1,0:T(8,128)(2,1)S(1)} %copy-done) | data formatting | bytes 2097152 | tf_op args[1]
  33.6 0.1 copy.36
  33.7 0.1 copy.23
  33.8 0.1 reshape.51
  34.0 0.2 select_reduce_fusion
  34.2 0.1 broadcast_add_fusion
  34.3 18.1 %collective-permute-done.2 = bf16[8,128,512]{2,1,0:T(8,128)(2,1)S(1)} collective-permute-done((bf16[8,128,512]{2,1,0:T(8,128)(2,1)S(1)}, bf16[8,128,512]{2,1,0:T(8,128)(2,1)S(1)}, u32[]{:S(2)}, u32[]{:S(2)}) %collective-permute-start.2) | collective-permute-done | bytes 1048608 | tf_op jit(solution)/shard_map/ppermute | solution.py:23
  52.5 1.0 copy-done.2
  53.5 21.5 %collective-permute-done.1 = bf16[8,128,512]{2,1,0:T(8,128)(2,1)} collective-permute-done((bf16[8,128,512]{2,1,0:T(8,128)(2,1)S(1)}, bf16[8,128,512]{2,1,0:T(8,128)(2,1)}, u32[]{:S(2)}, u32[]{:S(2)}) %collective-permute-start.1) | collective-permute-done | bytes 1048608 | tf_op jit(solution)/shard_map/ppermute | solution.py:22
  74.9 2.0 %pad_maximum_fusion = bf16[24,128,512]{2,1,0:T(8,128)(2,1)S(1)} fusion(bf16[8,128,512]{2,1,0:T(8,128)(2,1)} %copy-done.2, bf16[8,128,512]{2,1,0:T(8,128)(2,1)} %param.8, bf16[8,128,512]{2,1,0:T(8,128)(2,1)} %collective-permute-done.1), kind=kLoop, calls=%fused_computation.7 | loop fusion | flops 3145728 | bytes 6291456 | tf_op jit(solution)/shard_map/concatenate | solution.py:24
  77.0 2.8 %gather_fusion.1 = bf16[32,128,512]{2,1,0:T(8,128)(2,1)} fusion(bf16[24,128,512]{2,1,0:T(8,128)(2,1)S(1)} %pad_maximum_fusion, s32[1024]{0:T(1024)S(1)} %pad_clamp_fusion), kind=kCustom, calls=%fused_computation.1 | custom fusion | bytes 8388736 | tf_op jit(solution)/shard_map/gather | solution.py:57
  79.8 4.7 %multiply_reduce_fusion = f32[8,128,512]{2,1,0:T(8,128)} fusion(f32[8,4]{1,0:T(8,128)S(1)} %copy.36, bf16[32,128,512]{2,1,0:T(8,128)(2,1)} %gather_fusion.1), kind=kLoop, calls=%fused_computation.2 | loop fusion | flops 5767168 | bytes 6291584
  84.5 1.9 %copy.31 = f32[8,128,512]{1,2,0:T(8,128)S(1)} copy(f32[8,128,512]{2,1,0:T(8,128)} %multiply_reduce_fusion) | data formatting | bytes 4194304 | tf_op jit(solution)/shard_map/pc,pcab->pab/dot_general | solution.py:58
  86.4 1.6 %slice-done = bf16[2,1024,512]{2,1,0:T(8,128)(2,1)S(1)} async-done(((bf16[4,1024,512]{2,1,0:T(8,128)(2,1)}), bf16[2,1024,512]{2,1,0:T(8,128)(2,1)S(1)}, s32[]{:S(2)}) %slice-start) | async-done | bytes 2097176 | tf_op jit(solution)/shard_map/slice | solution.py:45
  88.1 5.9 %convert_bitcast_fusion = bf16[2,4,4,128,512]{3,4,0,1,2:T(8,128)(2,1)} fusion(bf16[4,4,256,512,1]{3,2,1,0,4:T(8,128)(2,1)} %bitcast.12, bf16[2,4,256,128,1]{3,2,1,0,4:T(8,128)(2,1)S(1)} %bitcast.13), kind=kOutput, calls=%fused_computation.6 | convolution fusion | flops 1075838976 | bytes 8912896 | tf_op jit(solution)/shard_map/igqa,jgqb->ijgab/dot_general | solution.py:49
  93.9 5.2 %gather_fusion = bf16[8,4,128,512]{2,3,1,0:T(8,128)(2,1)} fusion(bf16[2,4,4,128,512]{3,4,0,1,2:T(8,128)(2,1)} %convert_bitcast_fusion, s32[8]{0:T(128)S(1)} %fusion.10), kind=kCustom, calls=%fused_computation | custom fusion | bytes 8388672 | tf_op jit(solution)/shard_map/gather | solution.py:53
  99.2 3.2 %convert_reduce_fusion = f32[8,128,512]{1,2,0:T(8,128)S(1)} fusion(bf16[8,4,128,512]{2,3,1,0:T(8,128)(2,1)} %gather_fusion), kind=kLoop, calls=%fused_computation.3 | loop fusion | flops 3670016 | bytes 6291456 | tf_op jit(solution)/shard_map/reduce_sum | solution.py:54
  102.3 0.7 subtract_convert_fusion
  103.0 1.3 %copy.24 = bf16[8,128,512]{2,1,0:T(8,128)(2,1)} copy(bf16[8,128,512]{1,2,0:T(8,128)(2,1)S(1)} %subtract_convert_fusion) | data formatting | bytes 2097152 | tf_op jit(solution)/shard_map/convert_element_type | solution.py:68
  (24 shorter events, 0.3 us)
Async XLA Ops:
  6.5 19.0 %copy-start = (bf16[8,128,512]{2,1,0:T(8,128)(2,1)S(1)}, bf16[8,128,512]{2,1,0:T(8,128)(2,1)}, u32[]{:S(2)}) copy-start(bf16[8,128,512]{2,1,0:T(8,128)(2,1)} %param.8) | copy-start | bytes 3145732
  6.5 27.1 %copy-start.6 = (bf16[8,4]{0,1:T(4,128)(2,1)S(1)}, bf16[8,4]{0,1:T(4,128)(2,1)}, u32[]{:S(2)}) copy-start(bf16[8,4]{0,1:T(4,128)(2,1)} %param.11) | copy-start | bytes 196
  6.5 27.2 %copy-start.5 = (s32[8,4]{0,1:T(4,128)S(1)}, s32[8,4]{0,1:T(4,128)}, u32[]{:S(2)}) copy-start(s32[8,4]{0,1:T(4,128)} %param.10) | copy-start | bytes 388
  6.5 27.3 %copy-start.4 = (f32[512]{0:T(512)S(1)}, f32[512]{0:T(512)}, u32[]{:S(2)}) copy-start(f32[512]{0:T(512)} %param.12) | copy-start | bytes 6148
  6.5 27.4 %copy-start.3 = (s32[8,2]{0,1:T(2,128)S(1)}, s32[8,2]{0,1:T(2,128)}, u32[]{:S(2)}) copy-start(s32[8,2]{0,1:T(2,128)} %param.9) | copy-start | bytes 196
  6.5 27.4 %copy-start.7 = (f32[16]{0:T(128)S(1)}, f32[16]{0:T(128)}, u32[]{:S(2)}) copy-start(f32[16]{0:T(128)} %param.13) | copy-start | bytes 196
  6.6 79.9 %all-gather.2.cloned.1.call-start = ((), (), s32[]{:S(2)}) async-start(), calls=%async_computation | async-start | bytes 5242880 | tf_op jit(solution)/shard_map/all_gather | solution.py:40
  6.6 16.8 %collective-permute-start = (bf16[2,256,512]{2,1,0:T(8,128)(2,1)}, bf16[2,256,512]{2,1,0:T(8,128)(2,1)S(1)}, u32[]{:S(2)}, u32[]{:S(2)}) collective-permute-start(bf16[2,256,512]{2,1,0:T(8,128)(2,1)} %param.7), channel_id=1, source_target_pairs={{4,0},{8,4},{12,8},{16,12},{20,16},{24,20},{28,24},{5,1},{9,5},{13... | collective-permute-start | bytes 1572872 | tf_op jit(solution)/shard_map/ppermute | solution.py:12
  25.5 26.9 %collective-permute-start.2 = (bf16[8,128,512]{2,1,0:T(8,128)(2,1)S(1)}, bf16[8,128,512]{2,1,0:T(8,128)(2,1)S(1)}, u32[]{:S(2)}, u32[]{:S(2)}) collective-permute-start(bf16[8,128,512]{2,1,0:T(8,128)(2,1)S(1)} %copy-done), channel_id=1, source_target_pairs={{4,0},{8,4},{12,8},{16,12},{20,16},{24,20},{28,24},{5,1},{9,5},{13... | collective-permute-start | bytes 3145736 | tf_op jit(solution)/shard_map/ppermute | solution.py:23
  27.5 47.5 %collective-permute-start.1 = (bf16[8,128,512]{2,1,0:T(8,128)(2,1)S(1)}, bf16[8,128,512]{2,1,0:T(8,128)(2,1)}, u32[]{:S(2)}, u32[]{:S(2)}) collective-permute-start(bf16[8,128,512]{2,1,0:T(8,128)(2,1)S(1)} %copy-done), channel_id=1, source_target_pairs={{0,4},{4,8},{8,12},{12,16},{16,20},{20,24},{24,28},{1,5},{5,9},{9,... | collective-permute-start | bytes 3145736 | tf_op jit(solution)/shard_map/ppermute | solution.py:22
  52.5 1.0 copy-start.2
  86.4 1.6 %slice-start = ((bf16[4,1024,512]{2,1,0:T(8,128)(2,1)}), bf16[2,1024,512]{2,1,0:T(8,128)(2,1)S(1)}, s32[]{:S(2)}) async-start(bf16[4,1024,512]{2,1,0:T(8,128)(2,1)} %all-gather.2.cloned.1.call-done), calls=%async_computation.1 | async-start | bytes 4194304 | tf_op jit(solution)/shard_map/slice | solution.py:45
  99.2 3.2 %copy-start.1 = (bf16[8,128,512]{1,2,0:T(8,128)(2,1)S(1)}, bf16[8,128,512]{1,2,0:T(8,128)(2,1)}, u32[]{:S(2)}) copy-start(bf16[8,128,512]{1,2,0:T(8,128)(2,1)} %copy.20) | copy-start | bytes 3145732
Sparse Core Ops, SparseCore 0:
  25.6 34.6 all-gather.1
where the time goes:
time: 112 us; the launch traced here: 111 us
  waiting for transfers between devices  54.4 us (49%)
  local copies, waits for them, and re-layouts  15.6 us (14%)
  between operations  13.5 us (12%)
  other arithmetic  13 us (12%)
  starting transfers between devices  8.83 us (8%)
  matrix products  5.86 us (5%)
    ppermute x1, waiting for transfers between devices, extended_2(): before = lax.ppermute(last, axis, up)  21.5 us
    ppermute x1, waiting for transfers between devices, extended_2(): after = lax.ppermute(leading, axis, down)  18.1 us
    ppermute x1, waiting for transfers between devices, passed_along(): return lax.ppermute(block, axis, route)  14.7 us
    dot_general x1, matrix products, per_device(): jnp.einsum('igqa,jgqb->ijgab', left_split, right_split, preferred_element...  5.86 us
    gather x1, local copies, waits for them, and re-layouts, per_device(): picked_pairs = rounded[first_local, second_local]  5.21 us
    ppermute x1, starting transfers between devices, extended_2(): before = lax.ppermute(last, axis, up)  4.82 us
    unnamed x1, other arithmetic  4.71 us
    reduce_sum x1, other arithmetic, per_device(): integrals = jnp.sum(picked_pairs.astype(jnp.float32), axis=1)  3.17 us
  transfers between devices with their start and end apart: 4, of which 3 were waited for; matrix products, arithmetic and copies ran while one was open for 12% of the time, Pallas kernels for 0%

commit v1 on v0

v1 whole, which is shorter than its diff:
```python
import functools

import jax
import jax.numpy as jnp
from jax import lax
from jax.experimental import pallas as pl
from jax.experimental.pallas import tpu as pltpu
from jax.sharding import PartitionSpec as P

MESH = pl.DeviceIdType.MESH
damping = 0.7


def kernel(
    peers, groups, chunks,
    blocks, amps, pairs, coupling, fock, virtual, occupied,
    out,
    own, nxt, integrals, weights, column, result, *rest,
):
    parts = rest[:chunks]
    (own_sem, amp_sem, out_sem, nxt_send, nxt_recv, own_send, own_recv, far_send, far_recv,
     amp_send, amp_recv, fwd_send, fwd_recv) = rest[chunks:]
    orbitals, quarter, full = blocks.shape
    count, rows = amps.shape[:2]
    height = rows // chunks
    coupled_count = coupling.shape[1]
    o = lax.axis_index("orb")
    r = lax.axis_index("rep")
    even = lax.rem(o, 2) == 0
    has_prev, has_next = o > 0, o < peers - 1
    has_back2, has_on2 = o > 1, o < peers - 2
    partner = jnp.where(even, o + 1, o - 1)
    near_slot = jnp.where(even, 2 * count, 0)
    far_slot = jnp.where(even, 0, 2 * count)
    has_fwd = jnp.logical_or(jnp.logical_and(even, has_on2), jnp.logical_and(~even, has_back2))
    has_far = jnp.logical_or(jnp.logical_and(even, has_back2), jnp.logical_and(~even, has_on2))
    fwd_target = jnp.where(even, o + 2, o - 2)
    bits = [1 << b for b in reversed(range(groups.bit_length() - 1))]

    def remote(src, dst, send, recv, where):
        return pltpu.make_async_remote_copy(
            src_ref=src, dst_ref=dst, send_sem=send, recv_sem=recv, device_id=where, device_id_type=MESH
        )

    def flip(bit):
        return {"rep": jnp.where(lax.rem(r // bit, 2) == 0, r + bit, r - bit)}

    own_copy = pltpu.make_async_copy(blocks, own.at[0], own_sem)
    own_copy.start()
    amp_copies = [
        pltpu.make_async_copy(
            amps.at[:, pl.ds(k * height, height), :], parts[k].at[pl.ds(count, count)], amp_sem.at[k]
        )
        for k in range(chunks)
    ]
    for copy in amp_copies:
        copy.start()

    barrier = pltpu.get_barrier_semaphore()
    for bit in bits:
        pl.semaphore_signal(barrier, inc=1, device_id=flip(bit), device_id_type=MESH)
    for there, distance in ((has_prev, -1), (has_next, 1), (has_back2, -2), (has_on2, 2)):
        @pl.when(there)
        def _():
            pl.semaphore_signal(barrier, inc=1, device_id={"orb": o + distance}, device_id_type=MESH)
    ones = [jnp.where(there, 1, 0) for there in (has_prev, has_next, has_back2, has_on2)]
    pl.semaphore_wait(barrier, len(bits) + sum(ones))

    def block_copy(j):
        return remote(blocks.at[j], nxt.at[0, j], nxt_send.at[j], nxt_recv.at[j], {"orb": o - 1})

    def own_hop(m, bit, j):
        src = blocks.at[j] if m == 0 else own.at[m, j]
        return remote(src, own.at[m + bit, j], own_send.at[m + bit, j], own_recv.at[m + bit, j], flip(bit))

    def far_hop(m, bit, j):
        return remote(
            nxt.at[m, j], nxt.at[m + bit, j], far_send.at[m + bit, j], far_recv.at[m + bit, j], flip(bit)
        )

    def amp_copy(k):
        return remote(
            amps.at[:, pl.ds(k * height, height), :], parts[k].at[pl.ds(far_slot, count)],
            amp_send.at[k], amp_recv.at[k], {"orb": partner},
        )

    def amp_arrival(k):
        return remote(
            amps.at[:, pl.ds(k * height, height), :], parts[k].at[pl.ds(near_slot, count)],
            amp_send.at[k], amp_recv.at[k], {"orb": partner},
        )

    def fwd_copy(k):
        return remote(
            parts[k].at[pl.ds(near_slot, count)], parts[k].at[pl.ds(far_slot, count)],
            fwd_send.at[k], fwd_recv.at[k], {"orb": fwd_target},
        )

    hops, held = [], [0]
    for bit in bits:
        hops += [(m, bit) for m in held]
        held += [m + bit for m in held]

    @pl.when(has_prev)
    def _():
        for j in range(orbitals):
            block_copy(j).start()
    for m, bit in hops:
        if m == 0:
            for j in range(orbitals):
                own_hop(m, bit, j).start()
    for k in range(chunks):
        amp_copy(k).start()

    def forward(k):
        amp_arrival(k).wait_recv()

        @pl.when(has_fwd)
        def _():
            fwd_copy(k).start()

    @pl.when(has_next)
    def _():
        for j in range(orbitals):
            block_copy(j).wait_recv()
            for m, bit in hops:
                if m == 0:
                    far_hop(m, bit, j).start()

    weights[...] = fock[...].astype(jnp.float32)
    mine = virtual[:, pl.ds(pl.multiple_of(r * rows, rows), rows)]
    column[...] = jnp.transpose(jnp.broadcast_to(mine, (rows, rows)))
    own_copy.wait()
    arrivals = {m + bit: (m, bit) for m, bit in hops}
    later = {m: [(a, b) for a, b in hops if a == m] for m in range(1, groups)}

    def settle(hop, slot):
        m, bit = arrivals[slot]
        for j in range(orbitals):
            hop(m, bit, j).wait_recv()
            for a, b in later[slot]:
                hop(a, b, j).start()

    order = sorted(range(1, groups), key=lambda slot: [h for h in hops].index(arrivals[slot]))
    columns = pl.ds(pl.multiple_of(r * rows, rows), rows)

    def combos(right, i, shift):
        for j in range(orbitals):
            total = None
            for m in range(groups):
                product = lax.dot_general(
                    own[m, i, :, columns], right[m, j], (((0,), (0,)), ((), ())),
                    preferred_element_type=jnp.float32,
                )
                term = product.astype(jnp.bfloat16).astype(jnp.float32)
                total = term if total is None else total + term
            integrals[i * 2 * orbitals + shift + j] = total

    def far_slots():
        @pl.when(has_next)
        def _():
            for slot in order:
                settle(far_hop, slot)

    def far_combos(i):
        @pl.when(has_next)
        def _():
            combos(nxt, i, orbitals)

    for slot in order:
        settle(own_hop, slot)
    forward(0)
    for i in range(orbitals):
        combos(own, i, 0)
        forward(min(1 + i, chunks - 1)) if 1 + i < chunks else None
    sent = min(1 + orbitals, chunks)
    far_slots()
    for i in range(orbitals):
        if sent < chunks:
            forward(sent)
            sent += 1
        far_combos(i)

    base = o * orbitals
    first_pair = (o - 1) * count
    row = virtual[...]

    def finish(k):
        @pl.when(has_far)
        def _():
            fwd_copy(k).wait_recv()
        amp_copies[k].wait()
        spot = pl.ds(k * height, height)

        @pl.loop(0, count)
        def _(p):
            first, second = pairs[p, 0], pairs[p, 1]
            shift = occupied[first] + occupied[second]
            left, right = jnp.clip(first - base, 0, orbitals - 1), jnp.clip(second - base, 0, 2 * orbitals - 1)
            weight = weights[pl.ds(p, 1), :]
            coupled = None
            for c in range(coupled_count):
                place = jnp.clip(coupling[p, c] - first_pair, 0, 3 * count - 1)
                picked = parts[k][place].astype(jnp.float32)
                term = weight[:, c : c + 1] * picked
                coupled = term if coupled is None else coupled + term
            combo = left * 2 * orbitals + right
            residual = integrals[combo, spot, :] - coupled
            denominator = column[spot, 0:1] + row - shift
            previous = parts[k][count + p].astype(jnp.float32)
            updated = (1.0 - damping) * previous - damping * residual / denominator
            result[p, spot, :] = updated.astype(jnp.bfloat16)

        pltpu.make_async_copy(result.at[:, spot, :], out.at[:, spot, :], out_sem.at[k]).start()

    for k in range(chunks):
        while sent < min(chunks, k + 3):
            forward(sent)
            sent += 1
        finish(k)

    for k in range(chunks):
        spot = pl.ds(k * height, height)
        amp_copy(k).wait_send()
        pltpu.make_async_copy(result.at[:, spot, :], out.at[:, spot, :], out_sem.at[k]).wait()
    for m, bit in hops:
        for j in range(orbitals):
            own_hop(m, bit, j).wait_send()

    @pl.when(has_prev)
    def _():
        for j in range(orbitals):
            block_copy(j).wait_send()

    @pl.when(has_next)
    def _():
        for m, bit in hops:
            for j in range(orbitals):
                far_hop(m, bit, j).wait_send()

    @pl.when(has_fwd)
    def _():
        for k in range(chunks):
            fwd_copy(k).wait_send()


def solution(mesh):
    peers, groups = mesh.shape["orb"], mesh.shape["rep"]
    assert peers % 2 == 0 and groups & (groups - 1) == 0

    def per_device(blocks, amplitudes, pairs, coupling, fock, virtual, occupied):
        orbitals, quarter, full = blocks.shape
        count, rows, _ = amplitudes.shape
        chunks = rows // 16
        dma = pltpu.SemaphoreType.DMA
        vmem = pltpu.VMEM
        any_space = pl.BlockSpec(memory_space=pl.ANY)
        smem = pl.BlockSpec(memory_space=pltpu.SMEM)
        in_vmem = pl.BlockSpec(memory_space=pltpu.VMEM)
        return pl.pallas_call(
            functools.partial(kernel, peers, groups, chunks),
            out_shape=jax.ShapeDtypeStruct(amplitudes.shape, amplitudes.dtype),
            in_specs=[any_space, any_space, smem, smem, in_vmem, in_vmem, smem],
            out_specs=any_space,
            scratch_shapes=[
                vmem((groups, orbitals, quarter, full), jnp.bfloat16),
                vmem((groups, orbitals, quarter, full), jnp.bfloat16),
                vmem((2 * orbitals * orbitals, rows, full), jnp.float32),
                vmem(fock.shape, jnp.float32),
                vmem((rows, rows), jnp.float32),
                vmem((count, rows, full), jnp.bfloat16),
                *[vmem((3 * count, rows // chunks, full), jnp.bfloat16) for _ in range(chunks)],
                dma, dma((chunks,)), dma((chunks,)),
                dma((orbitals,)), dma((orbitals,)),
                dma((groups, orbitals)), dma((groups, orbitals)),
                dma((groups, orbitals)), dma((groups, orbitals)),
                dma((chunks,)), dma((chunks,)), dma((chunks,)), dma((chunks,)),
            ],
            compiler_params=pltpu.CompilerParams(
                collective_id=0, has_side_effects=True, vmem_limit_bytes=56 * 1024 * 1024
            ),
        )(blocks, amplitudes, pairs, coupling, fock, virtual.reshape(1, full), occupied)

    placed = (
        P("orb", "rep", None), P("orb", "rep", None), P("orb", None), P("orb", None), P("orb", None), P(), P(),
    )
    return jax.shard_map(
        per_device, mesh=mesh, in_specs=placed, out_specs=P("orb", "rep", None), check_vma=False
    )
```

time: 112 us -> 52.1 us (0.47)
  waiting for transfers between devices: 54.4 us -> 0 us
  Pallas kernels: 0 us -> 46.8 us
  between operations: 13.5 us -> 0.01 us
  other arithmetic: 13 us -> 0 us
  local copies, waits for them, and re-layouts: 15.6 us -> 4.97 us
  starting transfers between devices: 8.83 us -> 0 us
  matrix products: 5.86 us -> 0 us
    ppermute x3 -> x0, waiting for transfers between devices: 54.3 us -> none  [the longest x1 21.5 us: extended_2(): before = lax.ppermute(last, axis, up)]
    pallas_call x0 -> x1, Pallas kernels: none -> 46.8 us  [per_device(): pl.pallas_call(functools.partial(kernel, peers, groups, chunks), out_shap...]
    ppermute x3 -> x0, starting transfers between devices: 8.79 us -> none  [the longest x1 4.82 us: extended_2(): before = lax.ppermute(last, axis, up)]
    gather x2 -> x0, local copies, waits for them, and re-layouts: 8.01 us -> none  [the longest x1 5.21 us: per_device(): picked_pairs = rounded[first_local, second_local]]
    dot_general x1 -> x0, matrix products: 5.86 us -> none  [per_device(): jnp.einsum('igqa,jgqb->ijgab', left_split, right_split, preferred_element...]
    unnamed x1 -> x0, other arithmetic: 4.71 us -> none
    concatenate x3 -> x0, other arithmetic: 4.14 us -> none  [the longest x1 2.1 us: per_device(): extended = jnp.concatenate([blocks, next_blocks], axis=0)]
    reduce_sum x2 -> x0, other arithmetic: 3.35 us -> none  [the longest x1 3.17 us: per_device(): integrals = jnp.sum(picked_pairs.astype(jnp.float32), axis=1)]
  transfers between devices with their start and end apart: 4 -> 0, of which waited for: 3 -> 0; matrix products, arithmetic and copies ran while one was open for 12% -> 0% of each run, Pallas kernels for 0% -> 0%
where the time goes in v1:
time: 52.1 us; the launch traced here: 51.8 us
  Pallas kernels  46.8 us (90%)
  local copies, waits for them, and re-layouts  4.97 us (10%)
    pallas_call x1, Pallas kernels, per_device(): pl.pallas_call(functools.partial(kernel, peers, groups, chunks), out_shap...  46.8 us
    unnamed x10, local copies, waits for them, and re-layouts  4.97 us

profile of v1, /device:TPU:4, one launch (start us, length us, event | category | flops | bytes accessed | tf_op | source)
XLA Modules:
  0.0 51.8 jit_solution(9484478695401712989)
XLA Ops:
  0.0 0.0 copy-start.1
  0.0 0.7 %copy-done.1 = bf16[8,4]{0,1:T(4,128)(2,1)S(1)} copy-done((bf16[8,4]{0,1:T(4,128)(2,1)S(1)}, bf16[8,4]{0,1:T(4,128)(2,1)}, u32[]{:S(2)}) %copy-start.1) | copy-done | bytes 88
  0.7 0.0 copy-start.2
  0.7 0.7 %copy.10.fock = bf16[8,4]{1,0:T(8,128)(2,1)} copy(bf16[8,4]{0,1:T(4,128)(2,1)S(1)} %copy-done.1) | data formatting | bytes 128 | tf_op args[4]
  1.4 0.0 copy-done.2
  1.4 0.0 copy-start
  1.4 0.7 %copy.8.pairs = s32[8,2]{1,0:T(8,128)} copy(s32[8,2]{0,1:T(2,128)S(1)} %copy-done.2) | data formatting | bytes 128 | tf_op args[2]
  2.0 0.0 copy-done
  2.0 0.7 %copy.9.coupling = s32[8,4]{1,0:T(8,128)} copy(s32[8,4]{0,1:T(4,128)S(1)} %copy-done) | data formatting | bytes 256 | tf_op args[3]
  2.7 46.8 %shard_map.73 = bf16[8,128,512]{2,1,0:T(8,128)(2,1)} custom-call(bf16[2,256,512]{2,1,0:T(8,128)(2,1)} %blocks.1, bf16[8,128,512]{2,1,0:T(8,128)(2,1)} %amps.1, s32[8,2]{1,0:T(8,128)} %copy.8.pairs, s32[8,4]{1,0:T(8,128)} %copy.9.coupling, bf16[8,4]{1,0:T(8,128)(2,1)} %copy.10.fock, f32[1,512]{1,0:T(1,128)} %bitcast.1, f32[16]{0:T(128)} %occupied.1), custom_call_target="tpu_custom_call" | custom-call | tf_op jit(solution)/shard_map/pallas_call | solution.py:260
  49.6 2.3 %copy.12 = bf16[8,128,512]{2,1,0:T(8,128)(2,1)} copy(bf16[8,128,512]{2,1,0:T(8,128)(2,1)} %shard_map.73) | data formatting | bytes 2097152
Async XLA Ops:
  0.0 0.7 %copy-start.1 = (bf16[8,4]{0,1:T(4,128)(2,1)S(1)}, bf16[8,4]{0,1:T(4,128)(2,1)}, u32[]{:S(2)}) copy-start(bf16[8,4]{0,1:T(4,128)(2,1)} %param.11) | copy-start | bytes 196
  0.7 0.7 %copy-start.2 = (s32[8,2]{0,1:T(2,128)S(1)}, s32[8,2]{0,1:T(2,128)}, u32[]{:S(2)}) copy-start(s32[8,2]{0,1:T(2,128)} %param.9) | copy-start | bytes 196
  1.4 0.7 %copy-start = (s32[8,4]{0,1:T(4,128)S(1)}, s32[8,4]{0,1:T(4,128)}, u32[]{:S(2)}) copy-start(s32[8,4]{0,1:T(4,128)} %param.10) | copy-start | bytes 388

commit v2 on v1

--- a/solution.py
+++ b/solution.py
@@ -9,6 +9,8 @@
 
 MESH = pl.DeviceIdType.MESH
 damping = 0.7
+AHEAD = 1
+HEIGHT = 16
 
 
 def kernel(
@@ -23,7 +25,7 @@
     orbitals, quarter, full = blocks.shape
     count, rows = amps.shape[:2]
     height = rows // chunks
-    coupled_count = coupling.shape[1]
+    coupled_count = coupling.shape[0]
     o = lax.axis_index("orb")
     r = lax.axis_index("rep")
     even = lax.rem(o, 2) == 0
@@ -109,7 +111,8 @@
         if m == 0:
             for j in range(orbitals):
                 own_hop(m, bit, j).start()
-    for k in range(chunks):
+    issued = min(AHEAD, chunks)
+    for k in range(issued):
         amp_copy(k).start()
 
     def forward(k):
@@ -119,15 +122,23 @@
         def _():
             fwd_copy(k).start()
 
-    @pl.when(has_next)
-    def _():
-        for j in range(orbitals):
+    for j in range(orbitals):
+        @pl.when(has_prev)
+        def _():
+            block_copy(j).wait_send()
+        upto = chunks if j == orbitals - 1 else min(issued + 1, chunks)
+        for k in range(issued, upto):
+            amp_copy(k).start()
+        issued = upto
+
+        @pl.when(has_next)
+        def _():
             block_copy(j).wait_recv()
             for m, bit in hops:
                 if m == 0:
                     far_hop(m, bit, j).start()
 
-    weights[...] = fock[...].astype(jnp.float32)
+    weights[...] = jnp.transpose(fock[...].astype(jnp.float32))
     mine = virtual[:, pl.ds(pl.multiple_of(r * rows, rows), rows)]
     column[...] = jnp.transpose(jnp.broadcast_to(mine, (rows, rows)))
     own_copy.wait()
@@ -167,13 +178,21 @@
         def _():
             combos(nxt, i, orbitals)
 
-    for slot in order:
+    settle(own_hop, order[0])
+    forward(0)
+    sent = 1
+    for slot in order[1:]:
         settle(own_hop, slot)
-    forward(0)
+    forward(1)
+    sent = 2
     for i in range(orbitals):
         combos(own, i, 0)
-        forward(min(1 + i, chunks - 1)) if 1 + i < chunks else None
-    sent = min(1 + orbitals, chunks)
+        if sent < chunks:
+            forward(sent)
+            sent += 1
+    while sent < chunks // 2:
+        forward(sent)
+        sent += 1
     far_slots()
     for i in range(orbitals):
         if sent < chunks:
@@ -192,15 +211,15 @@
         amp_copies[k].wait()
         spot = pl.ds(k * height, height)
 
-        @pl.loop(0, count)
+        @pl.loop(0, count, unroll=True)
         def _(p):
-            first, second = pairs[p, 0], pairs[p, 1]
+            first, second = pairs[0, p], pairs[1, p]
             shift = occupied[first] + occupied[second]
             left, right = jnp.clip(first - base, 0, orbitals - 1), jnp.clip(second - base, 0, 2 * orbitals - 1)
             weight = weights[pl.ds(p, 1), :]
             coupled = None
             for c in range(coupled_count):
-                place = jnp.clip(coupling[p, c] - first_pair, 0, 3 * count - 1)
+                place = jnp.clip(coupling[c, p] - first_pair, 0, 3 * count - 1)
                 picked = parts[k][place].astype(jnp.float32)
                 term = weight[:, c : c + 1] * picked
                 coupled = term if coupled is None else coupled + term
@@ -227,11 +246,6 @@
         for j in range(orbitals):
             own_hop(m, bit, j).wait_send()
 
-    @pl.when(has_prev)
-    def _():
-        for j in range(orbitals):
-            block_copy(j).wait_send()
-
     @pl.when(has_next)
     def _():
         for m, bit in hops:
@@ -251,7 +265,7 @@
     def per_device(blocks, amplitudes, pairs, coupling, fock, virtual, occupied):
         orbitals, quarter, full = blocks.shape
         count, rows, _ = amplitudes.shape
-        chunks = rows // 16
+        chunks = rows // HEIGHT
         dma = pltpu.SemaphoreType.DMA
         vmem = pltpu.VMEM
         any_space = pl.BlockSpec(memory_space=pl.ANY)
@@ -279,7 +293,7 @@
             compiler_params=pltpu.CompilerParams(
                 collective_id=0, has_side_effects=True, vmem_limit_bytes=56 * 1024 * 1024
             ),
-        )(blocks, amplitudes, pairs, coupling, fock, virtual.reshape(1, full), occupied)
+        )(blocks, amplitudes, pairs.T, coupling.T, fock.T, virtual.reshape(1, full), occupied)
 
     placed = (
         P("orb", "rep", None), P("orb", "rep", None), P("orb", None), P("orb", None), P("orb", None), P(), P(),

time: 52.1 us -> 47.1 us (0.904)
  local copies, waits for them, and re-layouts: 4.97 us -> 2.26 us
  Pallas kernels: 46.8 us -> 44.7 us
    unnamed x10 -> x1, local copies, waits for them, and re-layouts: 4.97 us -> 2.26 us
    pallas_call x1, Pallas kernels: 46.8 us -> 44.7 us  [per_device(): pl.pallas_call(functools.partial(kernel, peers, groups, chunks), out_shap...]
where the time goes in v2:
time: 47.1 us; the launch traced here: 46.9 us
  Pallas kernels  44.7 us (95%)
  local copies, waits for them, and re-layouts  2.26 us (5%)
    pallas_call x1, Pallas kernels, per_device(): pl.pallas_call(functools.partial(kernel, peers, groups, chunks), out_shap...  44.7 us
    unnamed x1, local copies, waits for them, and re-layouts  2.26 us

profile of v2, /device:TPU:4, one launch (start us, length us, event | category | flops | bytes accessed | tf_op | source)
XLA Modules:
  0.0 46.9 jit_solution(14296222185988908974)
XLA Ops:
  0.0 44.7 %shard_map.73 = bf16[8,128,512]{2,1,0:T(8,128)(2,1)} custom-call(bf16[2,256,512]{2,1,0:T(8,128)(2,1)} %blocks.1, bf16[8,128,512]{2,1,0:T(8,128)(2,1)} %amps.1, s32[2,8]{1,0:T(2,128)} %bitcast.6, s32[4,8]{1,0:T(4,128)} %bitcast.4, bf16[4,8]{1,0:T(4,128)(2,1)} %bitcast.7, f32[1,512]{1,0:T(1,128)} %bitcast.5, f32[16]{0:T(128)} %occupied.1), custom_call_target="tpu_custom_call" | custom-call | tf_op jit(solution)/shard_map/pallas_call | solution.py:274
  44.7 2.3 %copy.9 = bf16[8,128,512]{2,1,0:T(8,128)(2,1)} copy(bf16[8,128,512]{2,1,0:T(8,128)(2,1)} %shard_map.73) | data formatting | bytes 2097152

commit v3 on v2

--- a/solution.py
+++ b/solution.py
@@ -107,13 +107,13 @@
     def _():
         for j in range(orbitals):
             block_copy(j).start()
-    for m, bit in hops:
-        if m == 0:
-            for j in range(orbitals):
-                own_hop(m, bit, j).start()
     issued = min(AHEAD, chunks)
     for k in range(issued):
         amp_copy(k).start()
+    for m, bit in hops:
+        if m == 0 and bit == bits[0]:
+            for j in range(orbitals):
+                own_hop(m, bit, j).start()
 
     def forward(k):
         amp_arrival(k).wait_recv()
@@ -138,6 +138,10 @@
                 if m == 0:
                     far_hop(m, bit, j).start()
 
+    for m, bit in hops:
+        if m == 0 and bit != bits[0]:
+            for j in range(orbitals):
+                own_hop(m, bit, j).start()
     weights[...] = jnp.transpose(fock[...].astype(jnp.float32))
     mine = virtual[:, pl.ds(pl.multiple_of(r * rows, rows), rows)]
     column[...] = jnp.transpose(jnp.broadcast_to(mine, (rows, rows)))
@@ -178,12 +182,11 @@
         def _():
             combos(nxt, i, orbitals)
 
+    forward(0)
     settle(own_hop, order[0])
-    forward(0)
-    sent = 1
+    forward(1)
     for slot in order[1:]:
         settle(own_hop, slot)
-    forward(1)
     sent = 2
     for i in range(orbitals):
         combos(own, i, 0)

time: 47.1 us -> 47.1 us (level)
  no operation moved by 1% of the time
where the time goes in v3:
time: 47.1 us; the launch traced here: 46.9 us
  Pallas kernels  44.7 us (95%)
  local copies, waits for them, and re-layouts  2.26 us (5%)
    pallas_call x1, Pallas kernels, per_device(): pl.pallas_call(functools.partial(kernel, peers, groups, chunks), out_shap...  44.7 us
    unnamed x1, local copies, waits for them, and re-layouts  2.26 us

profile of v3, /device:TPU:4, one launch (start us, length us, event | category | flops | bytes accessed | tf_op | source)
XLA Modules:
  0.0 46.9 jit_solution(6152280278998021219)
XLA Ops:
  0.0 44.7 %shard_map.73 = bf16[8,128,512]{2,1,0:T(8,128)(2,1)} custom-call(bf16[2,256,512]{2,1,0:T(8,128)(2,1)} %blocks.1, bf16[8,128,512]{2,1,0:T(8,128)(2,1)} %amps.1, s32[2,8]{1,0:T(2,128)} %bitcast.6, s32[4,8]{1,0:T(4,128)} %bitcast.4, bf16[4,8]{1,0:T(4,128)(2,1)} %bitcast.7, f32[1,512]{1,0:T(1,128)} %bitcast.5, f32[16]{0:T(128)} %occupied.1), custom_call_target="tpu_custom_call" | custom-call | tf_op jit(solution)/shard_map/pallas_call | solution.py:277
  44.7 2.3 %copy.9 = bf16[8,128,512]{2,1,0:T(8,128)(2,1)} copy(bf16[8,128,512]{2,1,0:T(8,128)(2,1)} %shard_map.73) | data formatting | bytes 2097152
